TPU v7x, 32 devices: a whole 2x2x4 slice. The times are simulated.
32 devices in a mesh: groups: 2 (over y), blk: 16 (over z, x, core).
Axes of the slice: x: 2, y: 2, z: 4, core: 2. Of those that a mesh axis runs over, the one named last changes fastest.
Arguments:
- particles: bfloat16 [4096, 32, 256], P(('groups', 'blk')), parts along dimension 0, may hold values from -6 to 6
- owner: int32 [4096, 1], P(('groups', 'blk')), parts along dimension 0, may hold values from 0 to 15; in each aligned block of 128 rows (0 to 127, 128 to 255, ...) at most 12 rows name the same one
- mic_local: int32 [4096], P(('groups', 'blk')), parts along dimension 0, may hold values from 0 to 5
- shifts: int32 [4096, 2], P(('groups', 'blk')), parts along dimension 0, may hold values from -5 to 5
- prior: int32 [4096], P(('groups', 'blk')), parts along dimension 0, may hold values from 0 to 9
- refs: bfloat16 [32, 32, 256], P(('groups', 'blk')), parts along dimension 0, may hold values from -8 to 8
- ctf: bfloat16 [192, 32, 128], P(('groups', 'blk')), parts along dimension 0, may hold values from -1 to 1
Outputs:
- posterior: float32 [4096, 16], P(('groups', 'blk')), parts along dimension 0
- evidence: float32 [4096], P(('groups', 'blk')), parts along dimension 0
- numer: float32 [32, 32, 256], P(('groups', 'blk')), parts along dimension 0
- denom: float32 [32, 32, 256], P(('groups', 'blk')), parts along dimension 0
There are 2 independent parts, one for each index of `groups`. A program takes and returns all parts, laid end to end along the dimension named above; each array names one. Nothing has to cross between parts.
Inputs may be any that keep to these rules, and one draw needn't show every extreme that they name: In the rows of one device no owner is named more than 12 times, a bound that some block reaches.
All inputs are finite; a program needn't handle non-finite values.
Results may differ from a plain program's by a relative error of at most 0.012.
Values may be sent and summed in bfloat16 or wider, within the bound.
A program may use at most 128 MiB of HBM per device.

v0:
```python
import math

import jax
import jax.numpy as jnp
from jax import lax
from jax.sharding import PartitionSpec as P

BOX = 128
ROTS = 36
MIC_DEV = 6


HIGH = lax.Precision.HIGHEST


def spectral_tables(angles, rotations):
    sample = jnp.arange(angles, dtype=jnp.float32)
    azimuth = 2.0 * jnp.pi * sample / angles
    order = jnp.where(sample < angles // 2, sample, sample - angles)
    phase = azimuth[:, None] * order[None, :]
    cosine = jnp.cos(phase)
    sine = jnp.sin(phase)
    forward = jnp.concatenate(
        [jnp.concatenate([cosine, -sine], 1), jnp.concatenate([sine, cosine], 1)], 0
    )
    turns = 2.0 * jnp.pi * jnp.arange(rotations, dtype=jnp.float32) / rotations
    spin = order[:, None] * turns[None, :]
    rotate = jnp.concatenate([jnp.cos(spin), jnp.sin(spin)], 0)
    return (forward, rotate, azimuth, order)


def turn_spectra(spectra, prior_steps, order):
    angles = order.shape[0]
    theta = 2.0 * jnp.pi * prior_steps.astype(jnp.float32) / 360.0
    spin = theta[:, None, None] * order[None, None, :]
    cosine = jnp.cos(spin)
    sine = jnp.sin(spin)
    real_part = spectra[..., :angles]
    imag_part = spectra[..., angles:]
    return jnp.concatenate(
        [real_part * cosine - imag_part * sine, real_part * sine + imag_part * cosine], -1
    )


def image_spectra(images, ctf_rows, offsets, prior_steps, forward, azimuth, order):
    angles = azimuth.shape[0]
    cycles = images.shape[1]
    values = images.astype(jnp.float32)
    real_part = values[..., :angles]
    imag_part = values[..., angles:]
    radius = jnp.arange(1, cycles + 1, dtype=jnp.float32)
    travel = (
        offsets[:, 0].astype(jnp.float32)[:, None] * jnp.cos(azimuth)[None, :]
        + offsets[:, 1].astype(jnp.float32)[:, None] * jnp.sin(azimuth)[None, :]
    )
    phase = -2.0 * jnp.pi / BOX * radius[None, :, None] * travel[:, None, :]
    cosine = jnp.cos(phase)
    sine = jnp.sin(phase)
    shifted = jnp.concatenate(
        [
            ctf_rows * (real_part * cosine - imag_part * sine),
            ctf_rows * (real_part * sine + imag_part * cosine),
        ],
        -1,
    )
    spectra = jnp.matmul(shifted, forward, precision=HIGH)
    return turn_spectra(spectra, prior_steps, order).astype(jnp.bfloat16)


def power_spectra(ctf_rows, forward):
    angles = ctf_rows.shape[-1]
    return jnp.matmul(ctf_rows * ctf_rows, forward[:angles], precision=HIGH)


def correlation(left, right):
    angles = left.shape[-1] // 2
    left_re = left[..., :angles]
    left_im = left[..., angles:]
    right_re = right[..., :angles]
    right_im = right[..., angles:]
    form = "ipm,kpm->ikm"
    real_sum = jnp.einsum(form, left_re, right_re, preferred_element_type=jnp.float32) + jnp.einsum(
        form, left_im, right_im, preferred_element_type=jnp.float32
    )
    imag_sum = jnp.einsum(form, left_re, right_im, preferred_element_type=jnp.float32) - jnp.einsum(
        form, left_im, right_re, preferred_element_type=jnp.float32
    )
    return jnp.concatenate([real_sum, imag_sum], -1)


def accumulate(spun, spectra):
    angles = spun.shape[-1] // 2
    spun_re = spun[..., :angles]
    spun_im = spun[..., angles:]
    spec_re = spectra[..., :angles]
    spec_im = spectra[..., angles:]
    form = "ikm,ipm->kpm"
    real_sum = jnp.einsum(form, spun_re, spec_re, preferred_element_type=jnp.float32) - jnp.einsum(
        form, spun_im, spec_im, preferred_element_type=jnp.float32
    )
    imag_sum = jnp.einsum(form, spun_re, spec_im, preferred_element_type=jnp.float32) + jnp.einsum(
        form, spun_im, spec_re, preferred_element_type=jnp.float32
    )
    return jnp.concatenate([real_sum, imag_sum], -1)


def slot_layout(target, devices, capacity):
    slots = devices * capacity
    hits = (target[:, None] == jnp.arange(devices, dtype=jnp.int32)[None, :]).astype(jnp.int32)
    earlier = jnp.cumsum(hits, axis=0) - hits
    position = target * capacity + jnp.sum(earlier * hits, axis=1)
    return jnp.arange(slots, dtype=jnp.int32)[:, None] == position[None, :]


def per_device(particles, owner, mic_local, shifts, prior, refs, ctf):
    devices = lax.axis_size("blk")
    local_count = particles.shape[0]
    cycles = particles.shape[1]
    angles = particles.shape[2] // 2
    class_local = refs.shape[0]
    classes = class_local * devices
    rotations = ROTS
    forward, rotate, azimuth, order = spectral_tables(angles, rotations)
    capacity = max(2, (3 * local_count + 2 * devices - 1) // (2 * devices))
    slots = devices * capacity
    placing = slot_layout(owner[:, 0], devices, capacity)
    outgoing = jnp.dot(
        placing.astype(jnp.bfloat16),
        particles.reshape(local_count, cycles * 2 * angles),
        preferred_element_type=jnp.float32,
    ).astype(jnp.bfloat16)
    labels = jnp.stack([mic_local, shifts[:, 0], shifts[:, 1], prior, jnp.ones_like(prior)], 1)
    out_labels = jnp.dot(placing.astype(jnp.int32), labels)
    arrived, arrived_labels = (
        lax.all_to_all(
            outgoing.reshape(devices, capacity, cycles, 2 * angles),
            "blk",
            split_axis=0,
            concat_axis=0,
            tiled=True,
        ),
        lax.all_to_all(
            out_labels.reshape(devices, capacity, 5), "blk", split_axis=0, concat_axis=0, tiled=True
        ),
    )
    arrived = arrived.reshape(slots, cycles, 2 * angles)
    arrived_labels = arrived_labels.reshape(slots, 5)
    filled = arrived_labels[:, 4].astype(jnp.float32)
    choose = (arrived_labels[:, 0:1] == jnp.arange(MIC_DEV, dtype=jnp.int32)[None, :]).astype(
        jnp.float32
    ) * filled[:, None]
    table = ctf.astype(jnp.float32)
    ctf_rows = jnp.dot(choose, table.reshape(MIC_DEV, cycles * angles), precision=HIGH).reshape(
        slots, cycles, angles
    )
    table_power = power_spectra(table, forward)
    row_power = jnp.dot(
        choose, table_power.reshape(MIC_DEV, cycles * 2 * angles), precision=HIGH
    ).reshape(slots, cycles, 2 * angles)
    spectra = image_spectra(
        arrived, ctf_rows, arrived_labels[:, 1:3], arrived_labels[:, 3], forward, azimuth, order
    )
    ctf_spectra = turn_spectra(row_power, arrived_labels[:, 3], order).astype(jnp.bfloat16)
    height = spectra.shape[0]
    values = lax.all_gather(refs, "blk", axis=0, tiled=True).astype(jnp.float32)
    ref_spectra = jnp.matmul(values, forward, precision=HIGH).astype(jnp.bfloat16)
    ref_power = values[..., :angles] ** 2 + values[..., angles:] ** 2
    ref_power_spectra = jnp.matmul(ref_power, forward[:angles], precision=HIGH).astype(jnp.bfloat16)
    ref_all = jnp.stack([ref_spectra, ref_power_spectra], 1)
    group = math.gcd(classes, 32)
    count_blocks = classes // group
    ref_blocks = ref_all.reshape(count_blocks, group, 2, cycles, 2 * angles)

    def score_block(block_refs):
        mixed = correlation(spectra, block_refs[:, 0]) - 0.5 * correlation(
            ctf_spectra, block_refs[:, 1]
        )
        fresh = jnp.matmul(mixed, rotate, precision=HIGH) / angles
        return fresh.reshape(height, group * rotations)

    scores = (
        lax.map(score_block, ref_blocks).transpose(1, 0, 2).reshape(height, classes * rotations)
    )
    peak = jnp.max(scores, axis=1, keepdims=True)
    expo = jnp.exp(scores - peak)
    total = jnp.sum(expo, axis=1, keepdims=True)
    weights = expo / total
    evidence = (peak + jnp.log(total))[:, 0]
    posterior = jnp.sum(weights.reshape(height, classes, rotations), axis=2)
    masked = weights * filled[:, None]
    unrotate = rotate.T
    block_weights_all = masked.reshape(height, count_blocks, group, rotations).transpose(1, 0, 2, 3)

    def one_group(block_weights):
        spun = jnp.matmul(block_weights, unrotate, precision=HIGH).astype(jnp.bfloat16)
        return jnp.stack([accumulate(spun, spectra), accumulate(spun, ctf_spectra)], 1)

    whole_terms = lax.map(one_group, block_weights_all).reshape(classes, 2, cycles, 2 * angles)
    sums = lax.psum_scatter(whole_terms, "blk", scatter_dimension=0, tiled=True)
    returned, returned_evidence = (
        lax.all_to_all(
            posterior.reshape(devices, capacity, classes).astype(jnp.bfloat16),
            "blk",
            split_axis=0,
            concat_axis=0,
            tiled=True,
        ).astype(jnp.float32),
        lax.all_to_all(
            evidence.reshape(devices, capacity).astype(jnp.bfloat16),
            "blk",
            split_axis=0,
            concat_axis=0,
            tiled=True,
        ).astype(jnp.float32),
    )
    unplace = placing.astype(jnp.float32).T
    posterior = jnp.dot(unplace, returned.reshape(slots, classes), precision=HIGH)
    evidence = jnp.dot(unplace, returned_evidence.reshape(slots, 1), precision=HIGH)[:, 0]
    return (posterior, evidence, sums[:, 0], sums[:, 1])


def solution(mesh):
    in_specs = (
        P(("groups", "blk"), None, None),
        P(("groups", "blk"), None),
        P(("groups", "blk")),
        P(("groups", "blk"), None),
        P(("groups", "blk")),
        P(("groups", "blk"), None, None),
        P(("groups", "blk"), None, None),
    )
    out_specs = (
        P(("groups", "blk"), None),
        P(("groups", "blk")),
        P(("groups", "blk"), None, None),
        P(("groups", "blk"), None, None),
    )
    return jax.shard_map(
        per_device, mesh=mesh, in_specs=in_specs, out_specs=out_specs, check_vma=False
    )
```

profile of v0, /device:TPU:0, one launch (start us, length us, event | category | flops | bytes accessed | tf_op | source)
XLA Modules:
  0.0 319.7 jit_solution(9420870486308753125)
XLA Ops:
  11.3 7.4 %all-to-all-start = ((s32[16,12,5]{1,2,0:T(8,128)}), s32[16,12,5]{1,2,0:T(8,128)S(1)}, u32[]{:S(2)}, u32[]{:S(2)}) async-start(s32[16,12,5]{1,2,0:T(8,128)} %copy.155), calls=%async_computation | async-start | bytes 131072 | tf_op jit(solution)/shard_map/all_to_all | solution.py:142
  18.7 3.0 copy.210
  25.6 5.9 %all-to-all-start.1 = ((bf16[16,12,32,256]{3,2,1,0:T(8,128)(2,1)}), bf16[16,12,32,256]{3,2,1,0:T(8,128)(2,1)}, u32[]{:S(2)}, u32[]{:S(2)}) async-start(bf16[16,12,32,256]{3,2,1,0:T(8,128)(2,1)} %bitcast.47), calls=%async_computation.1 | async-start | bytes 6291456 | tf_op jit(solution)/shard_map/all_to_all | solution.py:135
  31.5 68.4 %all_gather.3 = bf16[16,32,256]{2,1,0:T(8,128)(2,1)S(1)} all-gather(bf16[1,32,256]{2,1,0:T(8,128)(2,1)S(1)} %copy-done.20), channel_id=1, replica_groups=mesh['groups'=2,'blk'=16] {'blk'}, dimensions={0}, use_global_device_ids=true | all-gather | bytes 278528 | tf_op jit(solution)/shard_map/all_gather | solution.py:165
  108.7 5.2 %fusion.33 = f32[192,32,256]{2,0,1:T(8,128)S(1)} fusion(f32[192]{0:T(256)S(1)} %bitcast.142, s32[192]{0:T(256)S(1)} %bitcast.145, f32[1,6,32,256]{3,2,1,0:T(8,128)S(1)} %convolution_bitcast_fusion), kind=kOutput, calls=%fused_computation.79 | convolution fusion | flops 113248512 | bytes 6489600 | tf_op jit(solution)/shard_map/dot_general | solution.py:157
  120.0 15.4 %fusion.7 = (f32[192,32,128]{2,0,1:T(8,128)S(1)}, f32[192,32,128]{2,0,1:T(8,128)S(1)}) fusion(f32[192,32,128]{2,1,0:T(8,128)S(1)} %get-tuple-element.57, f32[192,32,128]{2,1,0:T(8,128)S(1)} %get-tuple-element.56, f32[192,128]{1,0:T(8,128)S(1)} %copy-done.15, f32[32]{0:T(128)S(1)} %add_multiply_fusion, bf16[1,6,32,128]{3,2,1,0:T(8,128)(2,1)S(1)} %bitcast.141, ...), kind=kOutput, calls=%fused_computation.13 | convolution fusion | flops 63703296 | bytes 12732032 | tf_op jit(solution)/shard_map/dot_general | solution.py:153
  136.2 8.4 %fusion = f32[192,32,256]{2,1,0:T(8,128)S(1)} fusion(f32[192,32,256]{2,0,1:T(8,128)S(1)} %pad_maximum_fusion, f32[128,128]{1,0:T(8,128)S(1)} %get-tuple-element.78, f32[128,128]{1,0:T(8,128)S(1)} %copy-done.18, f32[128,128]{1,0:T(8,128)S(1)} %get-tuple-element.76), kind=kOutput, calls=%fused_computation.2 | convolution fusion | flops 4832034816 | bytes 12779520 | tf_op jit(solution)/shard_map/dot_general | solution.py:66
  144.6 9.7 %add_convert_fusion = (bf16[192,32,128]{2,1,0:T(8,128)(2,1)}, bf16[192,32,128]{2,1,0:T(8,128)(2,1)}, bf16[192,32,128]{2,1,0:T(8,128)(2,1)}, bf16[192,32,128]{2,1,0:T(8,128)(2,1)}) fusion(f32[192,32,128]{2,0,1:T(8,128)S(1)} %copy-done.7, f32[192,32,128]{2,0,1:T(8,128)S(1)} %get-tuple-element.54, f32[192,128]{1,0:T(8,128)S(1)} %get-tuple-element.73, ...), kind=kLoop, calls=%fused_computation.17 | loop fusion | flops 12582912 | bytes 19070976 | tf_op jit(solution)/shard_map/while/body/eval_jaxpr/slice | solution.py:78
  154.4 3.7 %copy.171 = bf16[192,32,128]{0,1,2:T(8,128)(2,1)S(1)} copy(bf16[192,32,128]{2,1,0:T(8,128)(2,1)} %get-tuple-element.51) | data formatting | bytes 3145728 | tf_op jit(solution)/shard_map/while/body/eval_jaxpr/slice | solution.py:77
  158.1 4.8 %copy.173 = bf16[192,32,128]{0,1,2:T(8,128)(2,1)} copy(bf16[192,32,128]{2,1,0:T(8,128)(2,1)} %get-tuple-element.50) | data formatting | bytes 3145728 | tf_op jit(solution)/shard_map/while/body/eval_jaxpr/slice | solution.py:78
  169.1 4.8 %copy.161 = bf16[192,32,128]{0,1,2:T(8,128)(2,1)} copy(bf16[192,32,128]{2,1,0:T(8,128)(2,1)} %get-tuple-element.64) | data formatting | bytes 3145728 | tf_op jit(solution)/shard_map/while/body/eval_jaxpr/slice | solution.py:77
  173.9 4.8 %copy.163 = bf16[192,32,128]{0,1,2:T(8,128)(2,1)} copy(bf16[192,32,128]{2,1,0:T(8,128)(2,1)} %get-tuple-element.65) | data formatting | bytes 3145728 | tf_op jit(solution)/shard_map/while/body/eval_jaxpr/slice | solution.py:78
  185.3 3.0 maximum_subtract_fusion
  188.2 5.6 %copy.178 = f32[192,16,256]{2,1,0:T(8,128)} copy(f32[192,16,256]{0,1,2:T(8,128)} %maximum_subtract_fusion) | data formatting | bytes 6291456 | tf_op jit(solution)/shard_map/while/body/eval_jaxpr/sub | solution.py:175
  193.8 5.1 %fusion.70 = (f32[192]{0:T(256)S(1)}, f32[192,16,36]{2,1,0:T(8,128)S(1)}) fusion(f32[192,16,256]{2,1,0:T(8,128)} %copy.178, f32[128,36]{0,1:T(8,128)S(1)} %copy-done.19, f32[128,36]{0,1:T(8,128)S(1)} %get-tuple-element.74), kind=kOutput, calls=%fused_computation.126 | convolution fusion | flops 339968832 | bytes 3625728 | tf_op jit(solution)/shard_map/while/body/eval_jaxpr/dot_general | solution.py:178
  207.4 3.4 %fusion.77 = f32[128,32,16]{1,2,0:T(8,128)} fusion(bf16[192,32,128]{0,1,2:T(8,128)(2,1)} %copy.161, bf16[192,16,128]{0,1,2:T(8,128)(2,1)S(1)} %copy.184), kind=kOutput, calls=%fused_computation.133 | convolution fusion | flops 25165824 | bytes 2621440 | tf_op jit(solution)/shard_map/while/body/eval_jaxpr/ikm,ipm->kpm/dot_general | solution.py:98
  217.9 3.5 %fusion.16 = f32[16,32,128]{1,0,2:T(8,128)} fusion(f32[128,32,16]{1,2,0:T(8,128)} %fusion.77, bf16[192,32,128]{0,1,2:T(8,128)(2,1)} %copy.163, bf16[192,16,128]{0,1,2:T(8,128)(2,1)S(1)} %copy.186), kind=kOutput, calls=%fused_computation.38 | convolution fusion | flops 25231360 | bytes 2883584 | tf_op jit(solution)/shard_map/while/body/eval_jaxpr/ikm,ipm->kpm/dot_general | solution.py:98
  223.1 3.5 %fusion.15 = f32[16,32,128]{1,0,2:T(8,128)} fusion(f32[128,32,16]{1,2,0:T(8,128)} %fusion.78, bf16[192,32,128]{0,1,2:T(8,128)(2,1)} %copy.161, bf16[192,16,128]{0,1,2:T(8,128)(2,1)S(1)} %copy.186), kind=kOutput, calls=%fused_computation.36 | convolution fusion | flops 25231360 | bytes 2883584 | tf_op jit(solution)/shard_map/while/body/eval_jaxpr/ikm,ipm->kpm/dot_general | solution.py:101
  228.9 3.5 %fusion.14 = f32[16,32,128]{1,0,2:T(8,128)} fusion(f32[128,32,16]{1,2,0:T(8,128)} %fusion.79, bf16[192,32,128]{0,1,2:T(8,128)(2,1)} %copy.173, bf16[192,16,128]{0,1,2:T(8,128)(2,1)S(1)} %copy.186), kind=kOutput, calls=%fused_computation.34 | convolution fusion | flops 25231360 | bytes 2883584 | tf_op jit(solution)/shard_map/while/body/eval_jaxpr/ikm,ipm->kpm/dot_general | solution.py:98
  242.1 16.7 %all-to-all-start.3 = ((bf16[16,1,12]{2,1,0:T(2,128)(2,1)}), bf16[16,1,12]{2,1,0:T(2,128)(2,1)S(1)}, u32[]{:S(2)}, u32[]{:S(2)}) async-start(bf16[16,1,12]{2,1,0:T(2,128)(2,1)} %convert_element_type.98), calls=%async_computation.3 | async-start | bytes 16384 | tf_op jit(solution)/shard_map/all_to_all | solution.py:208
  260.6 4.5 %all-to-all-done.3 = bf16[16,1,12]{2,1,0:T(2,128)(2,1)S(1)} async-done(((bf16[16,1,12]{2,1,0:T(2,128)(2,1)}), bf16[16,1,12]{2,1,0:T(2,128)(2,1)S(1)}, u32[]{:S(2)}, u32[]{:S(2)}) %all-to-all-start.3) | async-done | bytes 416 | tf_op jit(solution)/shard_map/all_to_all | solution.py:208
  265.2 3.5 %all-to-all-start.2 = ((bf16[16,12,16]{1,2,0:T(8,128)(2,1)}), bf16[16,12,16]{1,2,0:T(8,128)(2,1)S(1)}, u32[]{:S(2)}, u32[]{:S(2)}) async-start(bf16[16,12,16]{1,2,0:T(8,128)(2,1)} %copy.180), calls=%async_computation.2 | async-start | bytes 131072 | tf_op jit(solution)/shard_map/all_to_all | solution.py:201
  269.5 6.1 %all-to-all-done.2 = bf16[16,12,16]{1,2,0:T(8,128)(2,1)S(1)} async-done(((bf16[16,12,16]{1,2,0:T(8,128)(2,1)}), bf16[16,12,16]{1,2,0:T(8,128)(2,1)S(1)}, u32[]{:S(2)}, u32[]{:S(2)}) %all-to-all-start.2) | async-done | bytes 6176 | tf_op jit(solution)/shard_map/all_to_all | solution.py:201
  276.4 34.6 %reduce-scatter.2.cloned.1.call-done = f32[1,2,32,256]{3,2,1,0:T(8,128)} async-done(((f32[16,2,32,256]{3,2,1,0:T(8,128)}), f32[1,2,32,256]{3,2,1,0:T(8,128)}) %reduce-scatter.2.cloned.1.call-update) | async-done | bytes 65552 | tf_op jit(solution)/shard_map/reduce_scatter | solution.py:199
  (123 shorter events, 70.3 us)
Async XLA Ops:
  9.6 12.1 %copy-start.21 = (s32[128]{0:T(128)}, s32[128]{0:T(128)S(1)}, u32[]{:S(2)}) copy-start(s32[128]{0:T(128)S(1)} %multiply_add_fusion.1) | copy-start | bytes 1540
  11.3 14.3 %all-to-all-start = ((s32[16,12,5]{1,2,0:T(8,128)}), s32[16,12,5]{1,2,0:T(8,128)S(1)}, u32[]{:S(2)}, u32[]{:S(2)}) async-start(s32[16,12,5]{1,2,0:T(8,128)} %copy.155), calls=%async_computation | async-start | bytes 131072 | tf_op jit(solution)/shard_map/all_to_all | solution.py:142
  25.6 5.9 %copy-start.20 = (bf16[1,32,256]{2,1,0:T(8,128)(2,1)S(1)}, bf16[1,32,256]{2,1,0:T(8,128)(2,1)}, u32[]{:S(2)}) copy-start(bf16[1,32,256]{2,1,0:T(8,128)(2,1)} %param.12) | copy-start | bytes 49156
  25.6 90.8 %all-to-all-start.1 = ((bf16[16,12,32,256]{3,2,1,0:T(8,128)(2,1)}), bf16[16,12,32,256]{3,2,1,0:T(8,128)(2,1)}, u32[]{:S(2)}, u32[]{:S(2)}) async-start(bf16[16,12,32,256]{3,2,1,0:T(8,128)(2,1)} %bitcast.47), calls=%async_computation.1 | async-start | bytes 6291456 | tf_op jit(solution)/shard_map/all_to_all | solution.py:135
  31.5 279.6 %reduce-scatter.2.cloned.1.call-start = ((), (), s32[]{:S(2)}) async-start(), calls=%async_computation.5 | async-start | bytes 1114112 | tf_op jit(solution)/shard_map/reduce_scatter | solution.py:199
  100.3 4.7 %copy-start.17 = (f32[128,128]{1,0:T(8,128)}, f32[128,128]{1,0:T(8,128)S(1)}, u32[]{:S(2)}) copy-start(f32[128,128]{1,0:T(8,128)S(1)} %get-tuple-element.77) | copy-start | bytes 196612
  100.9 5.4 %copy-start.16 = (bf16[6,32,128]{2,1,0:T(8,128)(2,1)S(1)}, bf16[6,32,128]{2,1,0:T(8,128)(2,1)}, u32[]{:S(2)}) copy-start(bf16[6,32,128]{2,1,0:T(8,128)(2,1)} %param.13) | copy-start | bytes 147460
  136.2 8.4 %copy-start.7 = (f32[192,32,128]{2,0,1:T(8,128)S(1)}, f32[192,32,128]{2,0,1:T(8,128)}, u32[]{:S(2)}) copy-start(f32[192,32,128]{2,0,1:T(8,128)} %get-tuple-element.55) | copy-start | bytes 9437188
  158.1 4.8 %copy-start.11 = (bf16[16,32,128]{1,0,2:T(8,128)(2,1)S(1)}, bf16[16,32,128]{1,0,2:T(8,128)(2,1)}, u32[]{:S(2)}) copy-start(bf16[16,32,128]{1,0,2:T(8,128)(2,1)} %copy.170) | copy-start | bytes 393220
  163.9 1.6 copy-start
  173.9 4.8 %copy-start.10 = (bf16[16,32,128]{1,0,2:T(8,128)(2,1)S(1)}, bf16[16,32,128]{1,0,2:T(8,128)(2,1)}, u32[]{:S(2)}) copy-start(bf16[16,32,128]{1,0,2:T(8,128)(2,1)} %copy.160) | copy-start | bytes 393220
  178.7 2.2 copy-start.2
  178.7 2.3 copy-start.12
  183.0 1.6 copy-start.8
  183.0 2.2 copy-start.9
  188.2 5.6 %copy-start.19 = (f32[128,36]{0,1:T(8,128)S(1)}, f32[128,36]{0,1:T(8,128)}, u32[]{:S(2)}) copy-start(f32[128,36]{0,1:T(8,128)} %get-tuple-element.75) | copy-start | bytes 55300
  198.9 5.0 %copy-start.5 = (f32[192,16,36]{2,1,0:T(8,128)}, f32[192,16,36]{2,1,0:T(8,128)S(1)}, u32[]{:S(2)}) copy-start(f32[192,16,36]{2,1,0:T(8,128)S(1)} %get-tuple-element.80) | copy-start | bytes 1327108
  207.4 3.4 %copy-start.4 = (bf16[192,32,128]{0,1,2:T(8,128)(2,1)S(1)}, bf16[192,32,128]{0,1,2:T(8,128)(2,1)}, u32[]{:S(2)}) copy-start(bf16[192,32,128]{0,1,2:T(8,128)(2,1)} %copy.163) | copy-start | bytes 4718596
  212.5 1.7 copy-start.1
  237.5 2.6 copy-start.14
  240.2 18.7 %copy-start.6 = (f32[192,16,36]{2,1,0:T(8,128)S(1)}, f32[192,16,36]{2,1,0:T(8,128)}, u32[]{:S(2)}) copy-start(f32[192,16,36]{2,1,0:T(8,128)} %copy-done.5) | copy-start | bytes 1327108
  240.2 28.6 %copy-start.22 = (s32[128]{0:T(128)S(1)}, s32[128]{0:T(128)}, u32[]{:S(2)}) copy-start(s32[128]{0:T(128)} %copy-done.21) | copy-start | bytes 1540
  242.1 23.1 %all-to-all-start.3 = ((bf16[16,1,12]{2,1,0:T(2,128)(2,1)}), bf16[16,1,12]{2,1,0:T(2,128)(2,1)S(1)}, u32[]{:S(2)}, u32[]{:S(2)}) async-start(bf16[16,1,12]{2,1,0:T(2,128)(2,1)} %convert_element_type.98), calls=%async_computation.3 | async-start | bytes 16384 | tf_op jit(solution)/shard_map/all_to_all | solution.py:208
  265.2 10.4 %all-to-all-start.2 = ((bf16[16,12,16]{1,2,0:T(8,128)(2,1)}), bf16[16,12,16]{1,2,0:T(8,128)(2,1)S(1)}, u32[]{:S(2)}, u32[]{:S(2)}) async-start(bf16[16,12,16]{1,2,0:T(8,128)(2,1)} %copy.180), calls=%async_computation.2 | async-start | bytes 131072 | tf_op jit(solution)/shard_map/all_to_all | solution.py:201
  (4 other events, 4.4 us)
Sparse Core Ops, SparseCore 0:
  241.5 69.4 reduce-scatter.1
where the time goes:
time: 325 us; the launch traced here: 320 us
  matrix products  71.4 us (22%)
  blocking collectives  68.4 us (21%)
  local copies, waits for them, and re-layouts  60.1 us (18%)
  waiting for transfers between devices  45.5 us (14%)
  starting transfers between devices  33.5 us (10%)
  other arithmetic  25.8 us (8%)
  between operations  15 us (5%)
    all_gather x1, blocking collectives, per_device(): values = lax.all_gather(refs, 'blk', axis=0, tiled=True).astype(jnp.float32)  68.4 us
    reduce_scatter x1, waiting for transfers between devices, per_device(): sums = lax.psum_scatter(whole_terms, 'blk', scatter_dimension=0, tiled=True)  34.6 us
    all_to_all x1, starting transfers between devices, per_device(): lax.all_to_all(evidence.reshape(devices, capacity).astype(jnp.bfloat16),...  16.7 us
    dot_general x1, matrix products, per_device(): jnp.dot(choose, table.reshape(MIC_DEV, cycles * angles), precision=HIGH)  15.4 us
    unnamed x48, local copies, waits for them, and re-layouts  10.8 us
    slice x1, other arithmetic, correlation(): left_im = left[..., angles:]  9.73 us
    slice x2, local copies, waits for them, and re-layouts, correlation(): left_im = left[..., angles:]  9.57 us
    slice x2, local copies, waits for them, and re-layouts, correlation(): left_re = left[..., :angles]  8.43 us
  transfers between devices with their start and end apart: 5, of which 4 were waited for; matrix products, arithmetic and copies ran while one was open for 8% of the time, Pallas kernels for 0%

commit v1 on v0

v1 whole, which is shorter than its diff:
```python
import functools

import jax
import jax.numpy as jnp
import numpy as np
from jax import lax
from jax.experimental import pallas as pl
from jax.experimental.pallas import tpu as pltpu
from jax.sharding import PartitionSpec as P

BOX = 128
ROTS = 36
ROWS = 40
SHIFT = 5
HIGH = lax.Precision.HIGHEST
MESH = pl.DeviceIdType.MESH
F32 = jnp.float32
BF16 = jnp.bfloat16
VMEM = pl.BlockSpec(memory_space=pltpu.VMEM)
SMEM = pl.BlockSpec(memory_space=pltpu.SMEM)
MIB = 1 << 20


def split_table(table):
    high = table.astype(np.float32).astype(BF16)
    low = (table - high.astype(np.float64)).astype(np.float32).astype(BF16)
    return high, low


def tables(angles, cycles):
    sample = np.arange(angles)
    order = np.where(sample < angles // 2, sample, sample - angles)
    phase = 2.0 * np.pi * ((sample[:, None] * order[None, :]) % angles) / angles
    cosine, sine = np.cos(phase), np.sin(phase)
    forward = np.block([[cosine, -sine], [sine, cosine]])
    spin = 2.0 * np.pi * ((order[:, None] * np.arange(ROTS)[None, :]) % ROTS) / ROTS
    rotate = np.zeros((2 * angles, ROWS))
    rotate[:, :ROTS] = np.concatenate([np.cos(spin), np.sin(spin)], 0)
    azimuth = 2.0 * np.pi * sample / angles
    step = np.arange(-SHIFT, SHIFT + 1)[:, None, None] * np.arange(1, cycles + 1)[None, :, None]
    moves = []
    for part in (np.cos(azimuth), np.sin(azimuth)):
        turn = -2.0 * np.pi / BOX * step * part[None, None, :]
        moves.append(np.concatenate([np.cos(turn), np.sin(turn)], -1).astype(np.float32))
    return forward, rotate, moves, order


def neighbours(devices):
    me = lax.axis_index("blk")
    core = lax.rem(me, 2)
    side = lax.rem(me // 2, 2)
    layer = me // 4
    return me, core, side, layer, devices // 4


def greet(partners):
    barrier = pltpu.get_barrier_semaphore()
    for partner in partners:
        pl.semaphore_signal(barrier, inc=1, device_id={"blk": partner}, device_id_type=MESH)
    pl.semaphore_wait(barrier, len(partners))


def gather_kernel(devices, own_ref, all_ref, send_sem, recv_sem):
    me, core, side, layer, layers = neighbours(devices)
    column = side * 2 + core
    across = (1 - side) * 2 + core
    sibling = me + 1 - 2 * core
    beside = me + 2 - 4 * side
    others = [lax.rem(layer + hop, layers) for hop in range(1, layers)]
    greet([other * 4 + column for other in others] + [sibling, beside])
    sent = []

    def send(source, block, target, slot):
        copy = pltpu.make_async_remote_copy(
            src_ref=source,
            dst_ref=all_ref.at[block],
            send_sem=send_sem.at[slot],
            recv_sem=recv_sem.at[block],
            device_id={"blk": target},
            device_id_type=MESH,
        )
        copy.start()
        sent.append(copy)

    def arrive(block):
        pltpu.make_async_remote_copy(
            src_ref=own_ref,
            dst_ref=all_ref.at[block],
            send_sem=send_sem.at[0],
            recv_sem=recv_sem.at[block],
            device_id={"blk": sibling},
            device_id_type=MESH,
        ).wait_recv()

    for hop, other in enumerate(others):
        send(own_ref, me, other * 4 + column, hop)
    send(own_ref, me, beside, layers)
    send(own_ref, me, sibling, 2 * layers)
    all_ref[me] = own_ref[...]
    far = me + 2 - 4 * side
    for hop in range(layers):
        if hop > 0:
            block = others[hop - 1] * 4 + column
            arrive(block)
            send(all_ref.at[block], block, beside, layers + hop)
            send(all_ref.at[block], block, sibling, 2 * layers + hop)
        far = (layer if hop == 0 else others[hop - 1]) * 4 + across
        arrive(far)
        send(all_ref.at[far], far, sibling, 3 * layers + hop)
    for hop in range(layers):
        place = (layer if hop == 0 else others[hop - 1]) * 4
        arrive(place + side * 2 + 1 - core)
        arrive(place + (1 - side) * 2 + 1 - core)
    for copy in sent:
        copy.wait_send()


def gather_blocks(own, devices):
    return pl.pallas_call(
        functools.partial(gather_kernel, devices),
        out_shape=jax.ShapeDtypeStruct((devices,) + own.shape, own.dtype),
        in_specs=[VMEM],
        out_specs=VMEM,
        scratch_shapes=[
            pltpu.SemaphoreType.DMA((devices,)),
            pltpu.SemaphoreType.DMA((devices,)),
        ],
        compiler_params=pltpu.CompilerParams(
            collective_id=0, has_side_effects=True, vmem_limit_bytes=48 * MIB
        ),
    )(own)


def reduce_kernel(devices, local, part_ref, numer_ref, denom_ref, *scratch):
    near, side_in, layer_in, side_out, layer_out, send_sem, near_sem, side_sem, layer_sem = scratch
    me, core, side, layer, layers = neighbours(devices)
    column = side * 2 + core
    sibling = me + 1 - 2 * core
    beside = me + 2 - 4 * side
    depth = part_ref.shape[0] // devices
    others = [lax.rem(layer + hop, layers) for hop in range(1, layers)]
    hops = list(range(1, layers)) + [0]
    greet([other * 4 + column for other in others] + [sibling, beside])

    def rows(block):
        return pl.ds(pl.multiple_of(block * depth, depth), depth)

    def target(hop):
        return layer if hop == 0 else others[hop - 1]

    def copy_to(source, sink, number, sem, device):
        return pltpu.make_async_remote_copy(
            src_ref=source,
            dst_ref=sink,
            send_sem=send_sem.at[number],
            recv_sem=sem,
            device_id={"blk": device},
            device_id_type=MESH,
        )

    first, second, third = {}, {}, {}
    for hop in hops:
        for flip in (1, 0):
            place = jnp.where(side == 1, 1 - flip, flip) if flip else side
            block = target(hop) * 4 + place * 2 + 1 - core
            slot = 2 * hop + flip
            first[slot] = copy_to(
                part_ref.at[rows(block)], near.at[slot], slot, near_sem.at[slot], sibling
            )
            first[slot].start()
    for hop in hops:
        first[2 * hop + 1].wait_recv()
        block = target(hop) * 4 + (1 - side) * 2 + core
        side_out[hop] = part_ref[rows(block), :] + near[2 * hop + 1]
        second[hop] = copy_to(
            side_out.at[hop], side_in.at[hop], 2 * layers + hop, side_sem.at[hop], beside
        )
        second[hop].start()
    for hop in hops:
        first[2 * hop].wait_recv()
        second[hop].wait_recv()
        block = target(hop) * 4 + column
        layer_out[hop] = part_ref[rows(block), :] + near[2 * hop] + side_in[hop]
        if hop:
            third[hop] = copy_to(
                layer_out.at[hop],
                layer_in.at[hop],
                3 * layers + hop,
                layer_sem.at[hop],
                target(hop) * 4 + column,
            )
            third[hop].start()
    total = layer_out[0]
    for hop in range(1, layers):
        third[hop].wait_recv()
        total = total + layer_in[hop]
    cycles, angles = numer_ref.shape[1], numer_ref.shape[2] // 2
    for item in range(local):
        turned = total[item * angles : (item + 1) * angles].T
        numer_ref[item, :, :angles] = turned[:cycles]
        denom_ref[item, :, :angles] = turned[cycles : 2 * cycles]
        numer_ref[item, :, angles:] = turned[2 * cycles : 3 * cycles]
        denom_ref[item, :, angles:] = turned[3 * cycles :]
    for copies in (first, second, third):
        for copy in copies.values():
            copy.wait_send()


def reduce_blocks(parts, devices, local, cycles, angles):
    layers = devices // 4
    depth = local * angles
    lanes = parts.shape[1]
    shape = jax.ShapeDtypeStruct((local, cycles, 2 * angles), F32)
    return pl.pallas_call(
        functools.partial(reduce_kernel, devices, local),
        out_shape=(shape, shape),
        in_specs=[VMEM],
        out_specs=(VMEM, VMEM),
        scratch_shapes=[
            pltpu.VMEM((2 * layers, depth, lanes), F32),
            pltpu.VMEM((layers, depth, lanes), F32),
            pltpu.VMEM((layers, depth, lanes), F32),
            pltpu.VMEM((layers, depth, lanes), F32),
            pltpu.VMEM((layers, depth, lanes), F32),
            pltpu.SemaphoreType.DMA((4 * layers,)),
            pltpu.SemaphoreType.DMA((2 * layers,)),
            pltpu.SemaphoreType.DMA((layers,)),
            pltpu.SemaphoreType.DMA((layers,)),
        ],
        compiler_params=pltpu.CompilerParams(
            collective_id=1, has_side_effects=True, vmem_limit_bytes=48 * MIB
        ),
    )(parts)


def halves(value):
    high = value.astype(BF16)
    return high, (value - high.astype(F32)).astype(BF16)


def dot(left, right):
    return jnp.dot(left, right, preferred_element_type=F32)


def dot_nt(left, right):
    return lax.dot_general(left, right, (((1,), (1,)), ((), ())), preferred_element_type=F32)


def score_kernel(sizes, index_ref, images_ref, all_ref, move_x_ref, move_y_ref, turn_ref,
                 forward_ref, rotate_ref, spread_ref, post_ref, evid_ref, parts_ref,
                 work, spec, refs):
    count, cycles, angles, classes, mics = sizes
    depth = 4 * cycles
    plane = cycles * count

    def shift_one(i):
        own, mic = index_ref[0, i], index_ref[1, i]
        move_x, move_y = move_x_ref[index_ref[2, i] + SHIFT], move_y_ref[index_ref[3, i] + SHIFT]
        row = pl.multiple_of(mic * cycles, cycles)
        transfer = all_ref[own, pl.ds(row, cycles), :].astype(F32)
        image = images_ref[i].astype(F32)
        x_re, x_im = move_x[:, :angles], move_x[:, angles:]
        y_re, y_im = move_y[:, :angles], move_y[:, angles:]
        re = x_re * y_re - x_im * y_im
        im = x_re * y_im + x_im * y_re
        a_re, a_im = image[:, :angles], image[:, angles:]
        work[pl.ds(i, cycles, stride=count), :] = transfer * (a_re * re - a_im * im)
        work[pl.ds(plane + i, cycles, stride=count), :] = transfer * (a_re * im + a_im * re)
        work[pl.ds(2 * plane + i, cycles, stride=count), :] = transfer * transfer

    @pl.loop(0, count // 4)
    def _(group):
        for u in range(4):
            shift_one(group * 4 + u)

    def place_ref(k):
        base = mics * cycles
        half = all_ref[k // sizes_local, pl.ds(base + (k % sizes_local) * angles, angles), :]
        value = half.astype(F32)
        lane = lax.broadcasted_iota(jnp.int32, value.shape, 1)
        swapped = pltpu.roll(value, depth // 2, 1)
        swapped = jnp.where(lane < depth // 2, swapped, -swapped)
        refs[pl.ds(k, angles, stride=2 * classes), :] = value
        refs[pl.ds(classes + k, angles, stride=2 * classes), :] = swapped

    sizes_local = classes // all_ref.shape[0]

    @pl.loop(0, classes // 2)
    def _(group):
        for u in range(2):
            place_ref(group * 2 + u)

    turn_re, turn_im = turn_ref[:angles], turn_ref[angles:]

    def put(values, start):
        re, im = values[:angles], values[angles:]
        spec[pl.ds(start, angles, stride=depth), :] = re * turn_re - im * turn_im
        spec[pl.ds(2 * cycles + start, angles, stride=depth), :] = re * turn_im + im * turn_re

    def transform(p):
        rows = pl.ds(pl.multiple_of(p * count, count), count)
        re = work[rows, :]
        im = work[pl.ds(pl.multiple_of(plane + p * count, count), count), :]
        power = work[pl.ds(pl.multiple_of(2 * plane + p * count, count), count), :]
        high, low = halves(jnp.concatenate([re, im], 1))
        f_high, f_low = forward_ref[0], forward_ref[1]
        values = dot_nt(f_high, high) + dot_nt(f_low, high) + dot_nt(f_high, low)
        put(values, p)
        high, low = halves(power)
        f_high, f_low = f_high[:, :angles], f_low[:, :angles]
        values = dot_nt(f_high, high) + dot_nt(f_low, high) + dot_nt(f_high, low)
        put(values, cycles + p)

    @pl.loop(0, cycles // 2)
    def _(group):
        for u in range(2):
            transform(group * 2 + u)

    def correlate(m):
        held = spec[pl.ds(pl.multiple_of(m * depth, depth), depth), :].astype(BF16)
        rows = pl.ds(pl.multiple_of(m * 2 * classes, 2 * classes), 2 * classes)
        parts_ref[pl.ds(m, 2 * classes, stride=angles), :] = dot(refs[rows, :].astype(BF16), held)

    @pl.loop(0, angles // 8)
    def _(group):
        for u in range(8):
            correlate(group * 8 + u)

    scale = 1.0 / angles
    valid = lax.broadcasted_iota(jnp.int32, (ROWS, count), 0) < ROTS

    def score(k, peak):
        re = parts_ref[pl.ds(pl.multiple_of(k * angles, angles), angles), :]
        im = parts_ref[pl.ds(pl.multiple_of((classes + k) * angles, angles), angles), :]
        high, low = halves(jnp.concatenate([re, im], 0))
        r_high, r_low = rotate_ref[0], rotate_ref[1]
        value = (dot(r_high, high) + dot(r_low, high) + dot(r_high, low)) * scale
        value = jnp.where(valid, value, -jnp.inf)
        work[pl.ds(pl.multiple_of(k * ROWS, 8), ROWS), :] = value
        return jnp.maximum(peak, value)

    def score_two(group, peak):
        return score(group * 2 + 1, score(group * 2, peak))

    peak = lax.fori_loop(0, classes // 2, score_two, jnp.full((ROWS, count), -jnp.inf, F32))
    peak = jnp.max(peak, axis=0, keepdims=True)

    def expo(k, total):
        rows = pl.ds(pl.multiple_of(k * ROWS, 8), ROWS)
        value = jnp.exp(work[rows, :] - peak)
        work[rows, :] = value
        return total + value

    total = lax.fori_loop(0, classes, expo, jnp.zeros((ROWS, count), F32))
    total = jnp.sum(total, axis=0, keepdims=True)
    evid_ref[...] = peak + jnp.log(total)
    share = 1.0 / total

    def unrotate(k):
        weights = work[pl.ds(pl.multiple_of(k * ROWS, 8), ROWS), :] * share
        post_ref[pl.ds(k, 1), :] = jnp.sum(weights, axis=0, keepdims=True)
        high, low = halves(weights)
        stacked = jnp.concatenate(
            [high.astype(F32), high.astype(F32), low.astype(F32), jnp.zeros((8, count), F32)], 0
        ).astype(BF16)
        value = dot(spread_ref[...], stacked)
        refs[pl.ds(k, angles, stride=2 * classes), :] = value[:angles]
        refs[pl.ds(classes + k, angles, stride=2 * classes), :] = value[angles:]

    @pl.loop(0, classes // 2)
    def _(group):
        for u in range(2):
            unrotate(group * 2 + u)

    def gather_up(m):
        held = spec[pl.ds(pl.multiple_of(m * depth, depth), depth), :]
        other = jnp.concatenate([-held[depth // 2 :], held[: depth // 2]], 0)
        right = jnp.concatenate([held, other], 1).astype(BF16)
        rows = pl.ds(pl.multiple_of(m * 2 * classes, 2 * classes), 2 * classes)
        spun = refs[rows, :]
        left = jnp.concatenate([spun[:classes], spun[classes:]], 1).astype(BF16)
        parts_ref[pl.ds(m, classes, stride=angles), :] = dot_nt(left, right)

    @pl.loop(0, angles // 8)
    def _(group):
        for u in range(8):
            gather_up(group * 8 + u)


def per_device(particles, owner, mic_local, shifts, prior, refs, ctf):
    devices = lax.axis_size("blk")
    count, cycles, angles = particles.shape[0], particles.shape[1], particles.shape[2] // 2
    local = refs.shape[0]
    classes = local * devices
    mics = ctf.shape[0]
    forward, rotate, moves, order = tables(angles, cycles)

    values = refs.astype(F32)
    table = jnp.asarray(forward.astype(np.float32))
    spectra = jnp.matmul(values, table, precision=HIGH).astype(BF16)
    power = values[..., :angles] ** 2 + values[..., angles:] ** 2
    power_spectra = jnp.matmul(power, table[:angles], precision=HIGH).astype(BF16)
    both = jnp.stack([spectra, -0.5 * power_spectra], 1).reshape(local, 2, cycles, 2, angles)
    both = both.transpose(0, 4, 3, 1, 2).reshape(local * angles, 4 * cycles)
    own = jnp.concatenate([ctf.reshape(mics * cycles, angles), both.astype(BF16)], 0)
    everything = gather_blocks(own, devices)

    index = jnp.stack([owner[:, 0], mic_local, shifts[:, 0], shifts[:, 1]])
    theta = 2.0 * jnp.pi * prior.astype(F32) / 360.0
    spin = jnp.asarray(order.astype(np.float32))[:, None] * theta[None, :]
    turn = jnp.concatenate([jnp.cos(spin), jnp.sin(spin)], 0)
    forward_t = jnp.asarray(np.stack(split_table(forward.T)))
    rotate_high, rotate_low = split_table(rotate)
    rotate_t = jnp.asarray(np.stack([rotate_high.T, rotate_low.T]))
    spread = jnp.asarray(
        np.concatenate(
            [rotate_high, rotate_low, rotate_high, np.zeros((2 * angles, 8), BF16)], 1
        )
    )
    post, evidence, parts = pl.pallas_call(
        functools.partial(score_kernel, (count, cycles, angles, classes, mics)),
        out_shape=(
            jax.ShapeDtypeStruct((classes, count), F32),
            jax.ShapeDtypeStruct((1, count), F32),
            jax.ShapeDtypeStruct((2 * classes * angles, 4 * cycles), F32),
        ),
        in_specs=[SMEM] + [VMEM] * 8,
        out_specs=(VMEM, VMEM, VMEM),
        scratch_shapes=[
            pltpu.VMEM((3 * cycles * count, angles), F32),
            pltpu.VMEM((angles * 4 * cycles, count), F32),
            pltpu.VMEM((2 * classes * angles, count), F32),
        ],
        compiler_params=pltpu.CompilerParams(vmem_limit_bytes=63 * MIB),
    )(index, particles, everything, jnp.asarray(moves[0]), jnp.asarray(moves[1]), turn,
      forward_t, rotate_t, spread)
    numer, denom = reduce_blocks(parts[: classes * angles], devices, local, cycles, angles)
    return post.T, evidence[0], numer, denom


def solution(mesh):
    in_specs = (
        P(("groups", "blk"), None, None),
        P(("groups", "blk"), None),
        P(("groups", "blk")),
        P(("groups", "blk"), None),
        P(("groups", "blk")),
        P(("groups", "blk"), None, None),
        P(("groups", "blk"), None, None),
    )
    out_specs = (
        P(("groups", "blk"), None),
        P(("groups", "blk")),
        P(("groups", "blk"), None, None),
        P(("groups", "blk"), None, None),
    )
    return jax.shard_map(
        per_device, mesh=mesh, in_specs=in_specs, out_specs=out_specs, check_vma=False
    )
```

time: 325 us -> 91 us (0.28); the launches traced: 320 us -> 90.6 us
  Pallas kernels: 0 us -> 78.1 us
  matrix products: 71.4 us -> 2.26 us
  blocking collectives: 68.4 us -> 0 us
  local copies, waits for them, and re-layouts: 60.1 us -> 4.48 us
  waiting for transfers between devices: 45.5 us -> 0 us
  starting transfers between devices: 33.5 us -> 0 us
  other arithmetic: 25.8 us -> 5.08 us
  between operations: 15 us -> 0.72 us
    pallas_call x0 -> x3, Pallas kernels: none -> 78.1 us  [the longest x1 39.2 us: per_device(): pl.pallas_call(functools.partial(score_kernel, (count, cycles, angles, cl...]
    dot_general x28 -> x2, matrix products: 71.4 us -> 2.26 us  [the longest x1 1.17 us: per_device(): spectra = jnp.matmul(values, table, precision=HIGH).astype(BF16)]
    all_gather x1 -> x0, blocking collectives: 68.4 us -> none  [per_device(): values = lax.all_gather(refs, 'blk', axis=0, tiled=True).astype(jnp.float32)]
    reduce_scatter x1 -> x0, waiting for transfers between devices: 34.6 us -> none  [per_device(): sums = lax.psum_scatter(whole_terms, 'blk', scatter_dimension=0, tiled=True)]
    all_to_all x4 -> x0, starting transfers between devices: 33.5 us -> none  [the longest x1 16.7 us: per_device(): lax.all_to_all(evidence.reshape(devices, capacity).astype(jnp.bfloat16),...]
    slice x15 -> x1, local copies, waits for them, and re-layouts: 31.8 us -> 1.29 us  [per_device(): parts[:classes * angles]]
    all_to_all x4 -> x0, waiting for transfers between devices: 10.9 us -> none  [the longest x1 6.05 us: per_device(): lax.all_to_all(posterior.reshape(devices, capacity, classes).astype(jnp.b...]
    slice x1 -> x0, other arithmetic: 9.73 us -> none  [correlation(): left_im = left[..., angles:]]
  transfers between devices with their start and end apart: 5 -> 0, of which waited for: 4 -> 0; matrix products, arithmetic and copies ran while one was open for 8% -> 0% of each run, Pallas kernels for 0% -> 0%
where the time goes in v1:
time: 91 us; the launch traced here: 90.6 us
  Pallas kernels  78.1 us (86%)
  other arithmetic  5.08 us (6%)
  local copies, waits for them, and re-layouts  4.48 us (5%)
  matrix products  2.26 us (2%)
    pallas_call x1, Pallas kernels, per_device(): pl.pallas_call(functools.partial(score_kernel, (count, cycles, angles, cl...  39.2 us
    pallas_call x1, Pallas kernels, gather_blocks(): pl.pallas_call(functools.partial(gather_kernel, devices), out_shape=jax.S...  22.8 us
    pallas_call x1, Pallas kernels, reduce_blocks(): pl.pallas_call(functools.partial(reduce_kernel, devices, local), out_shap...  16 us
    unnamed x4, local copies, waits for them, and re-layouts  2.28 us

profile of v1, /device:TPU:0, one launch (start us, length us, event | category | flops | bytes accessed | tf_op | source)
XLA Modules:
  0.0 90.6 jit_solution(15058717536546207518)
XLA Ops:
  0.6 0.7 convert_multiply_fusion
  1.3 0.8 slice_bitcast_fusion.1
  2.0 1.3 %pad_add_fusion.index_ref = s32[4,128]{1,0:T(4,128)} fusion(s32[1,128]{1,0:T(1,128)S(1)} %get-tuple-element.17, s32[1,128]{1,0:T(1,128)S(1)} %get-tuple-element.16, s32[1,128]{1,0:T(1,128)} %bitcast.24, s32[1,128]{1,0:T(1,128)} %bitcast.25), kind=kLoop, calls=%fused_computation.14 | loop fusion | flops 1536 | bytes 4096 | tf_op jit(solution)/shard_map/stack | solution.py:408
  3.3 1.2 %fusion = bf16[32,256]{1,0:T(8,128)(2,1)S(1)} fusion(f32[256,256]{1,0:T(8,128)} %constant.21.clone, bf16[1,32,256]{2,1,0:T(8,128)(2,1)} %param.19), kind=kOutput, calls=%fused_computation.2 | convolution fusion | flops 25174016 | bytes 294912 | tf_op jit(solution)/shard_map/dot_general | solution.py:400
  4.5 0.7 convert_element_type.15
  5.2 1.1 %fusion.1 = bf16[32,256]{1,0:T(8,128)(2,1)S(1)} fusion(f32[128,256]{1,0:T(8,128)} %constant.30, f32[1,32,256]{2,1,0:T(8,128)S(1)} %convert_element_type.15), kind=kOutput, calls=%fused_computation.3 | convolution fusion | flops 12611584 | bytes 180224 | tf_op jit(solution)/shard_map/dot_general | solution.py:402
  6.4 0.1 copy.22
  6.5 0.8 pad_maximum_fusion.1.own_ref
  7.3 1.0 %multiply_cosine_fusion = (f32[128,128]{1,0:T(8,128)S(1)}, f32[128,128]{1,0:T(8,128)S(1)}) fusion(f32[128]{0:T(128)S(1)} %convert_multiply_fusion, f32[128]{0:T(128)} %constant.22.clone), kind=kLoop, calls=%fused_computation.6 | loop fusion | flops 16384 | bytes 132096 | tf_op jit(solution)/shard_map/cos | solution.py:411
  8.3 0.7 pad_maximum_fusion.turn_ref
  8.9 22.8 %shard_map.165.all_ref = bf16[16,320,128]{2,1,0:T(8,128)(2,1)S(1)} custom-call(bf16[320,128]{1,0:T(8,128)(2,1)S(1)} %pad_maximum_fusion.1.own_ref), custom_call_target="tpu_custom_call" | custom-call | tf_op jit(solution)/shard_map/pallas_call | solution.py:119
  31.7 0.0 copy-start
  31.8 1.0 %copy-done = bf16[16,320,128]{2,1,0:T(8,128)(2,1)} copy-done((bf16[16,320,128]{2,1,0:T(8,128)(2,1)}, bf16[16,320,128]{2,1,0:T(8,128)(2,1)S(1)}, u32[]{:S(2)}) %copy-start) | copy-done | bytes 1310744
  32.8 39.2 %shard_map.166 = (f32[16,128]{1,0:T(8,128)}, f32[1,128]{1,0:T(1,128)}, f32[4096,128]{1,0:T(8,128)}) custom-call(s32[4,128]{1,0:T(4,128)} %pad_add_fusion.index_ref, bf16[128,32,256]{2,1,0:T(8,128)(2,1)} %images_ref.1, bf16[16,320,128]{2,1,0:T(8,128)(2,1)} %copy-done, f32[11,32,256]{2,1,0:T(8,128)} %constant.26.clone.move_x_ref, ...), custom_call_target="tpu_custom_call" | custom-call | tf_op jit(solution)/shard_map/pallas_call | solution.py:420
  72.0 1.3 %slice.23.part_ref = f32[2048,128]{1,0:T(8,128)S(1)} slice(f32[4096,128]{1,0:T(8,128)} %get-tuple-element.11), slice={[0:2048], [0:128]} | slice | bytes 2097152 | tf_op jit(solution)/shard_map/slice | solution.py:437
  73.3 16.0 %shard_map.167 = (f32[1,32,256]{2,1,0:T(8,128)S(1)}, f32[1,32,256]{2,1,0:T(8,128)S(1)}) custom-call(f32[2048,128]{1,0:T(8,128)S(1)} %slice.23.part_ref), custom_call_target="tpu_custom_call" | custom-call | tf_op jit(solution)/shard_map/pallas_call | solution.py:214
  89.4 0.6 copy.25
  90.0 0.6 copy.26
  (5 shorter events, 0.0 us)
Async XLA Ops:
  31.7 1.1 %copy-start = (bf16[16,320,128]{2,1,0:T(8,128)(2,1)}, bf16[16,320,128]{2,1,0:T(8,128)(2,1)S(1)}, u32[]{:S(2)}) copy-start(bf16[16,320,128]{2,1,0:T(8,128)(2,1)S(1)} %shard_map.165.all_ref) | copy-start | bytes 3932164

commit v2 on v1

--- a/solution.py
+++ b/solution.py
@@ -19,6 +19,8 @@
 VMEM = pl.BlockSpec(memory_space=pltpu.VMEM)
 SMEM = pl.BlockSpec(memory_space=pltpu.SMEM)
 MIB = 1 << 20
+PAD = 8
+CHUNKS = 4
 
 
 def split_table(table):
@@ -41,7 +43,7 @@
     moves = []
     for part in (np.cos(azimuth), np.sin(azimuth)):
         turn = -2.0 * np.pi / BOX * step * part[None, None, :]
-        moves.append(np.concatenate([np.cos(turn), np.sin(turn)], -1).astype(np.float32))
+        moves.append(np.concatenate([np.cos(turn), np.sin(turn)], -1))
     return forward, rotate, moves, order
 
 
@@ -387,12 +389,457 @@
             gather_up(group * 8 + u)
 
 
+def fused_kernel(sizes, owner_ref, mic_ref, shift_ref, images_ref, ctf_ref, own_values_ref,
+                 prior_ref, moves_ref, turns_ref, forward_ref, power_ref,
+                 rotate_ref, spread_ref, post_ref, evid_ref, numer_ref, denom_ref,
+                 all_ctf, all_refs, own_refs, work, table, phase, spec, refs, mixed, parts,
+                 near, side_out, side_in, layer_out, layer_in,
+                 ctf_send, ctf_recv, refs_send, refs_recv, near_sems, side_sems, layer_sems):
+    devices, count, cycles, angles = sizes
+    classes = devices
+    depth = 4 * cycles
+    lane_rows, deep, pairs, tall = count + PAD, depth + PAD, 2 * classes + PAD, angles + PAD
+    plane = cycles * lane_rows
+    chunk = angles // CHUNKS
+    wide = chunk + PAD
+
+    me, core, side, layer, layers = neighbours(devices)
+    column = side * 2 + core
+    sibling = me + 1 - 2 * core
+    beside = me + 2 - 4 * side
+    others = [lax.rem(layer + hop, layers) for hop in range(1, layers)]
+    places = [layer] + others
+    greet([other * 4 + column for other in others] + [sibling, beside])
+    waiting = []
+
+    def push(source, sink, send_sem, recv_sem, device):
+        copy = pltpu.make_async_remote_copy(
+            src_ref=source,
+            dst_ref=sink,
+            send_sem=send_sem,
+            recv_sem=recv_sem,
+            device_id={"blk": device},
+            device_id_type=MESH,
+        )
+        copy.start()
+        waiting.append(copy)
+        return copy
+
+    def spreader(own, everything, sends, recvs):
+        def send(source, block, device, slot):
+            push(source, everything.at[block], sends.at[slot], recvs.at[block], device)
+
+        def arrive(block):
+            pltpu.make_async_remote_copy(
+                src_ref=own,
+                dst_ref=everything.at[block],
+                send_sem=sends.at[0],
+                recv_sem=recvs.at[block],
+                device_id={"blk": sibling},
+                device_id_type=MESH,
+            ).wait_recv()
+
+        def begin():
+            for hop, other in enumerate(others):
+                send(own, me, other * 4 + column, hop)
+            send(own, me, beside, layers)
+            send(own, me, sibling, 2 * layers)
+
+        def along(hop):
+            block = places[hop] * 4 + column
+            arrive(block)
+            send(everything.at[block], block, beside, layers + hop)
+            send(everything.at[block], block, sibling, 2 * layers + hop)
+
+        def over(hop):
+            block = places[hop] * 4 + (1 - side) * 2 + core
+            arrive(block)
+            send(everything.at[block], block, sibling, 3 * layers + hop)
+
+        def finish():
+            for place in places:
+                arrive(place * 4 + side * 2 + 1 - core)
+                arrive(place * 4 + (1 - side) * 2 + 1 - core)
+
+        return begin, along, over, finish
+
+    ctf_begin, ctf_along, ctf_over, ctf_finish = spreader(ctf_ref, all_ctf, ctf_send, ctf_recv)
+    refs_begin, refs_along, refs_over, refs_finish = spreader(
+        own_refs, all_refs, refs_send, refs_recv
+    )
+
+    ctf_begin()
+    all_ctf[me] = ctf_ref[...]
+    f_high, f_low = forward_ref[0], forward_ref[1]
+    values = own_values_ref[0].astype(F32)
+    v_re, v_im = values[:, :angles], values[:, angles:]
+    halved = -0.5 * (v_re * v_re + v_im * v_im)
+    none = jnp.zeros_like(halved)
+    stacked = jnp.concatenate(
+        [
+            values,
+            jnp.concatenate([halved, none], 1),
+            jnp.concatenate([v_im, -v_re], 1),
+            jnp.concatenate([none, -halved], 1),
+        ],
+        0,
+    )
+    high, low = halves(stacked)
+    top, bottom = f_high[:angles], f_low[:angles]
+    own_block = (dot_nt(top, high) + dot_nt(bottom, high) + dot_nt(top, low)).astype(BF16)
+    own_refs[...] = own_block
+    all_refs[me] = own_block
+    refs_begin()
+
+    def spread_image(i):
+        image = images_ref[i].astype(F32)
+        work[pl.ds(i, cycles, stride=lane_rows), :] = image[:, :angles]
+        work[pl.ds(plane + i, cycles, stride=lane_rows), :] = image[:, angles:]
+
+    def picks(rows, line):
+        return (lax.broadcasted_iota(jnp.int32, (rows, count), 0) == line).astype(F32)
+
+    step_x, step_y = picks(16, shift_ref[0:1] + SHIFT), picks(16, shift_ref[1:2] + SHIFT)
+    blank = jnp.zeros((32, count), F32)
+    moved = jnp.concatenate([step_x] * 3 + [step_y] * 3 + [blank], 0).T.astype(BF16)
+    moved = dot(moved, moves_ref[...])
+    x_re, x_im = moved[:, :angles], moved[:, angles : 2 * angles]
+    y_re, y_im = moved[:, 2 * angles : 3 * angles], moved[:, 3 * angles :]
+    for slot in (0, 2):
+        phase[slot] = x_re * y_re - x_im * y_im
+        phase[slot + 1] = x_re * y_im + x_im * y_re
+    mics = ctf_ref.shape[0] // cycles
+    held_rows = table.shape[0] // (cycles + PAD)
+    picked = picks(held_rows, owner_ref[...] * mics + mic_ref[...]).T.astype(BF16)
+
+    steps = max(layers, 1)
+    span = count // steps
+
+    for hop in range(steps):
+
+        @pl.loop(0, span // 4)
+        def _(group):
+            for u in range(4):
+                spread_image(hop * span + group * 4 + u)
+
+        if hop + 1 < layers:
+            ctf_along(hop + 1)
+    for hop in range(layers):
+        ctf_over(hop)
+    for hop in range(1, layers):
+        refs_along(hop)
+
+    chosen = picks(16, prior_ref[...])
+    chosen = jnp.concatenate([chosen, chosen, chosen, jnp.zeros_like(chosen)], 0).astype(BF16)
+    turn = dot(turns_ref[...], chosen)
+    turn_re, turn_im = turn[:angles], turn[angles:]
+    ctf_finish()
+
+    table[...] = jnp.zeros_like(table)
+
+    @pl.loop(0, devices)
+    def _(block):
+        for mic in range(mics):
+            row = pl.multiple_of((block * mics + mic) * (cycles + PAD), 8)
+            rows = all_ctf[block, mic * cycles : (mic + 1) * cycles, :]
+            table[pl.ds(row, cycles), :] = rows.astype(F32)
+
+    def put(values, start):
+        re, im = values[:angles], values[angles:]
+        spec[pl.ds(start, angles, stride=deep), :] = re * turn_re - im * turn_im
+        spec[pl.ds(2 * cycles + start, angles, stride=deep), :] = re * turn_im + im * turn_re
+
+    def transform(p):
+        lines, powers = [], []
+        w_re, w_im = phase[2], phase[3]
+        t_re, t_im = phase[0], phase[1]
+        for u in range(2):
+            row = pl.multiple_of((p + u) * lane_rows, 8)
+            scale = dot(picked, table[pl.ds(p + u, held_rows, stride=cycles + PAD), :].astype(BF16))
+            a_re = work[pl.ds(row, count), :] * scale
+            a_im = work[pl.ds(pl.multiple_of(plane + (p + u) * lane_rows, 8), count), :] * scale
+            re, im = a_re * t_re - a_im * t_im, a_re * t_im + a_im * t_re
+            t_re, t_im = t_re * w_re - t_im * w_im, t_re * w_im + t_im * w_re
+            lines.append(jnp.concatenate([re, im], 1))
+            powers.append(scale * scale)
+        phase[0] = t_re
+        phase[1] = t_im
+        high, low = halves(jnp.concatenate(lines, 0))
+        values = dot_nt(forward_ref[0], high) + dot_nt(forward_ref[1], high)
+        values = values + dot_nt(forward_ref[0], low)
+        put(values[:, :count], p)
+        put(values[:, count:], p + 1)
+        high, low = halves(jnp.concatenate(powers, 0))
+        both = power_ref[...]
+        values = dot_nt(both, jnp.concatenate([high, high], 1))
+        values = values + dot_nt(both[:, :angles], low)
+        put(values[:, :count], cycles + p)
+        put(values[:, count:], cycles + p + 1)
+
+    part = cycles // steps
+    for hop in range(steps):
+
+        @pl.loop(0, part // 2)
+        def _(group):
+            transform(hop * part + group * 2)
+
+        refs_over(hop)
+    refs_finish()
+
+    def position(k):
+        return (k % 2) * (classes // 2) + ((k // 2) % 2) * (classes // 4) + k // 4
+
+    def place_ref(k):
+        value = all_refs[k].astype(F32)
+        lane = lax.broadcasted_iota(jnp.int32, value.shape, 1)
+        swapped = pltpu.roll(value, depth // 2, 1)
+        swapped = jnp.where(lane < depth // 2, swapped, -swapped)
+        refs[pl.ds(position(k), angles, stride=pairs), :] = value
+        refs[pl.ds(classes + position(k), angles, stride=pairs), :] = swapped
+
+    @pl.loop(0, classes // 2)
+    def _(group):
+        for u in range(2):
+            place_ref(group * 2 + u)
+
+    def correlate(m):
+        held = spec[pl.ds(pl.multiple_of(m * deep, 8), depth), :].astype(BF16)
+        rows = pl.ds(pl.multiple_of(m * pairs, 8), 2 * classes)
+        mixed[pl.ds(m, 2 * classes, stride=tall), :] = dot(refs[rows, :].astype(BF16), held)
+
+    @pl.loop(0, angles // 8)
+    def _(group):
+        for u in range(8):
+            correlate(group * 8 + u)
+
+    valid = lax.broadcasted_iota(jnp.int32, (ROWS, count), 0) < ROTS
+
+    def score(k, peak):
+        re = mixed[pl.ds(pl.multiple_of(k * tall, 8), angles), :]
+        im = mixed[pl.ds(pl.multiple_of((classes + k) * tall, 8), angles), :]
+        high, low = halves(jnp.concatenate([re, im], 0))
+        r_high, r_low = rotate_ref[0], rotate_ref[1]
+        value = (dot(r_high, high) + dot(r_low, high) + dot(r_high, low)) * (1.0 / angles)
+        value = jnp.where(valid, value, -jnp.inf)
+        work[pl.ds(pl.multiple_of(k * ROWS, 8), ROWS), :] = value
+        return jnp.maximum(peak, value)
+
+    def score_four(group, peak):
+        for u in range(4):
+            peak = score(group * 4 + u, peak)
+        return peak
+
+    peak = lax.fori_loop(0, classes // 4, score_four, jnp.full((ROWS, count), -jnp.inf, F32))
+    peak = jnp.max(peak, axis=0, keepdims=True)
+
+    def expo(k, total):
+        rows = pl.ds(pl.multiple_of(k * ROWS, 8), ROWS)
+        value = jnp.exp(work[rows, :] - peak)
+        work[rows, :] = value
+        return total + value
+
+    total = lax.fori_loop(0, classes, expo, jnp.zeros((ROWS, count), F32))
+    total = jnp.sum(total, axis=0, keepdims=True)
+    evid_ref[...] = peak + jnp.log(total)
+    share = 1.0 / total
+
+    def unrotate(k):
+        row = position(k)
+        weights = work[pl.ds(pl.multiple_of(row * ROWS, 8), ROWS), :] * share
+        post_ref[pl.ds(k, 1), :] = jnp.sum(weights, axis=0, keepdims=True)
+        high, low = halves(weights)
+        stacked = jnp.concatenate(
+            [high.astype(F32), high.astype(F32), low.astype(F32), jnp.zeros((8, count), F32)], 0
+        ).astype(BF16)
+        value = dot(spread_ref[...], stacked)
+        refs[pl.ds(row, angles, stride=pairs), :] = value[:angles]
+        refs[pl.ds(classes + row, angles, stride=pairs), :] = value[angles:]
+
+    @pl.loop(0, classes // 4)
+    def _(group):
+        for u in range(4):
+            unrotate(group * 4 + u)
+
+    def gather_up(number, step):
+        m = number * chunk + step
+        held = spec[pl.ds(pl.multiple_of(m * deep, 8), depth), :]
+        other = jnp.concatenate([-held[depth // 2 :], held[: depth // 2]], 0)
+        right = jnp.concatenate([held, other], 1).astype(BF16)
+        spun = refs[pl.ds(pl.multiple_of(m * pairs, 8), 2 * classes), :]
+        left = jnp.concatenate([spun[:classes], spun[classes:]], 1).astype(BF16)
+        parts.at[number][pl.ds(step, classes, stride=wide), :] = dot_nt(left, right)
+
+    half, quarter = classes // 2 * wide, classes // 4 * wide
+
+    def near_rows(number, flip, place):
+        place = pl.multiple_of(flip * quarter + place * wide, 8)
+        mine = pl.multiple_of(core * half + place, 8)
+        return parts[number, pl.ds(mine, chunk), :] + near[number, pl.ds(place, chunk), :]
+
+    first, second, third = {}, {}, {}
+
+    def stage_near(number):
+        start = pl.multiple_of((1 - core) * half, 8)
+        first[number] = push(
+            parts.at[number, pl.ds(start, half)],
+            near.at[number],
+            near_sems.at[0, number],
+            near_sems.at[1, number],
+            sibling,
+        )
+
+    def stage_side(number):
+        first[number].wait_recv()
+        for place in range(layers):
+            side_out[number, place] = near_rows(number, 1 - side, place)
+        second[number] = push(
+            side_out.at[number],
+            side_in.at[number],
+            side_sems.at[0, number],
+            side_sems.at[1, number],
+            beside,
+        )
+
+    def stage_layer(number):
+        second[number].wait_recv()
+        for hop, place in enumerate(places):
+            layer_out[number, hop] = near_rows(number, side, place) + side_in[number, place]
+            if hop:
+                third[number, hop] = push(
+                    layer_out.at[number, hop],
+                    layer_in.at[number, hop],
+                    layer_sems.at[0, number, hop],
+                    layer_sems.at[1, number, hop],
+                    place * 4 + column,
+                )
+
+    def stage_total(number):
+        total = layer_out[number, 0]
+        for hop in range(1, layers):
+            third[number, hop].wait_recv()
+            total = total + layer_in[number, hop]
+        return total
+
+    parts[...] = jnp.zeros_like(parts)
+    for number in range(CHUNKS):
+
+        @pl.loop(0, chunk // 8)
+        def _(group):
+            for u in range(8):
+                gather_up(number, group * 8 + u)
+
+        stage_near(number)
+        if number >= 1:
+            stage_side(number - 1)
+        if number >= 2:
+            stage_layer(number - 2)
+    stage_side(CHUNKS - 1)
+    if CHUNKS >= 2:
+        stage_layer(CHUNKS - 2)
+    stage_layer(CHUNKS - 1)
+    turned = jnp.concatenate([stage_total(number) for number in range(CHUNKS)], 0).T
+    numer_ref[0, :, :angles] = turned[:cycles]
+    denom_ref[0, :, :angles] = turned[cycles : 2 * cycles]
+    numer_ref[0, :, angles:] = turned[2 * cycles : 3 * cycles]
+    denom_ref[0, :, angles:] = turned[3 * cycles :]
+    for copy in waiting:
+        copy.wait_send()
+
+
+def three(values):
+    pieces = []
+    rest = values.astype(np.float64)
+    for _ in range(3):
+        piece = rest.astype(np.float32).astype(BF16)
+        pieces.append(piece)
+        rest = rest - piece.astype(np.float64)
+    return pieces
+
+
+def run_fused(particles, owner, mic_local, shifts, prior, refs, ctf, devices):
+    count, cycles, angles = particles.shape[0], particles.shape[1], particles.shape[2] // 2
+    classes = devices
+    layers = devices // 4
+    mics = ctf.shape[0]
+    depth = 4 * cycles
+    forward, rotate, moves, order = tables(angles, cycles)
+    chunk = angles // CHUNKS
+    wide = chunk + PAD
+    forward_high, forward_low = split_table(forward.T)
+    rotate_high, rotate_low = split_table(rotate)
+    rows = -(-devices * mics // 128) * 128
+    theta = 2.0 * np.pi * np.arange(16) / 360.0
+    spin = order[:, None] * theta[None, :]
+    turns = np.concatenate([np.cos(spin), np.sin(spin)], 0)
+    moving = np.zeros((128, 4 * angles), np.float32).astype(BF16)
+    for axis in range(2):
+        found = three(moves[axis][:, 0])
+        for number, piece in enumerate(found):
+            start = 48 * axis + 16 * number
+            moving[start : start + 2 * SHIFT + 1, axis * 2 * angles :][:, : 2 * angles] = piece
+    pieces = three(turns)
+    constants = (
+        moving,
+        np.concatenate(pieces + [np.zeros_like(pieces[0])], 1),
+        np.stack([forward_high, forward_low]),
+        np.concatenate([forward_high[:, :angles], forward_low[:, :angles]], 1),
+        np.stack([rotate_high.T, rotate_low.T]),
+        np.concatenate(
+            [rotate_high, rotate_low, rotate_high, np.zeros((2 * angles, 8), BF16)], 1
+        ),
+    )
+    sums = jax.ShapeDtypeStruct((1, cycles, 2 * angles), F32)
+    dma = pltpu.SemaphoreType.DMA
+    post, evidence, numer, denom = pl.pallas_call(
+        functools.partial(fused_kernel, (devices, count, cycles, angles)),
+        out_shape=(
+            jax.ShapeDtypeStruct((classes, count), F32),
+            jax.ShapeDtypeStruct((1, count), F32),
+            sums,
+            sums,
+        ),
+        in_specs=[VMEM] * 13,
+        out_specs=(VMEM,) * 4,
+        scratch_shapes=[
+            pltpu.VMEM((devices, mics * cycles, angles), BF16),
+            pltpu.VMEM((devices, angles, depth), BF16),
+            pltpu.VMEM((angles, depth), BF16),
+            pltpu.VMEM((2 * cycles * (count + PAD), angles), F32),
+            pltpu.VMEM((rows * (cycles + PAD), angles), F32),
+            pltpu.VMEM((4, count, angles), F32),
+            pltpu.VMEM((angles * (depth + PAD), count), F32),
+            pltpu.VMEM((angles * (2 * classes + PAD), count), F32),
+            pltpu.VMEM((2 * classes * (angles + PAD), count), F32),
+            pltpu.VMEM((CHUNKS, classes * wide, depth), F32),
+            pltpu.VMEM((CHUNKS, classes // 2 * wide, depth), F32),
+            pltpu.VMEM((CHUNKS, layers, chunk, depth), F32),
+            pltpu.VMEM((CHUNKS, layers, chunk, depth), F32),
+            pltpu.VMEM((CHUNKS, layers, chunk, depth), F32),
+            pltpu.VMEM((CHUNKS, layers, chunk, depth), F32),
+            dma((devices,)),
+            dma((devices,)),
+            dma((devices,)),
+            dma((devices,)),
+            dma((2, CHUNKS)),
+            dma((2, CHUNKS)),
+            dma((2, CHUNKS, layers)),
+        ],
+        compiler_params=pltpu.CompilerParams(
+            collective_id=2, has_side_effects=True, vmem_limit_bytes=60 * MIB
+        ),
+    )(owner.reshape(1, count), mic_local.reshape(1, count), shifts.T, particles, ctf.reshape(mics * cycles, angles), refs,
+      prior.reshape(1, count), *[jnp.asarray(constant) for constant in constants])
+    return post.T, evidence[0], numer, denom
+
+
 def per_device(particles, owner, mic_local, shifts, prior, refs, ctf):
     devices = lax.axis_size("blk")
     count, cycles, angles = particles.shape[0], particles.shape[1], particles.shape[2] // 2
     local = refs.shape[0]
     classes = local * devices
     mics = ctf.shape[0]
+    if local == 1 and classes <= 32:
+        return run_fused(particles, owner, mic_local, shifts, prior, refs, ctf, devices)
     forward, rotate, moves, order = tables(angles, cycles)
 
     values = refs.astype(F32)
@@ -432,7 +879,7 @@
             pltpu.VMEM((2 * classes * angles, count), F32),
         ],
         compiler_params=pltpu.CompilerParams(vmem_limit_bytes=63 * MIB),
-    )(index, particles, everything, jnp.asarray(moves[0]), jnp.asarray(moves[1]), turn,
+    )(index, particles, everything, jnp.asarray(moves[0], F32), jnp.asarray(moves[1], F32), turn,
       forward_t, rotate_t, spread)
     numer, denom = reduce_blocks(parts[: classes * angles], devices, local, cycles, angles)
     return post.T, evidence[0], numer, denom

time: 91 us -> 60.9 us (0.67)
  Pallas kernels: 78.1 us -> 54.7 us
  other arithmetic: 5.08 us -> 0 us
  matrix products: 2.26 us -> 0 us
    pallas_call x3 -> x1, Pallas kernels: 78.1 us -> 54.7 us  [run_fused(): pl.pallas_call(functools.partial(fused_kernel, (devices, count, cycles, a...]
    unnamed x4, local copies, waits for them, and re-layouts: 2.28 us -> 5.15 us
    dot_general x2 -> x0, matrix products: 2.26 us -> none  [the longest x1 1.17 us: per_device(): spectra = jnp.matmul(values, table, precision=HIGH).astype(BF16)]
    concatenate x2 -> x0, other arithmetic: 1.47 us -> none  [the longest x1 0.82 us: per_device(): jnp.concatenate([ctf.reshape(mics * cycles, angles), both.astype(BF16)], 0)]
    slice x1 -> x0, local copies, waits for them, and re-layouts: 1.29 us -> none  [per_device(): parts[:classes * angles]]
    another operation x2 -> x0, other arithmetic: 1.27 us -> none  [the longest x1 1.26 us: per_device(): index = jnp.stack([owner[:, 0], mic_local, shifts[:, 0], shifts[:, 1]])]
    cos x1 -> x0, other arithmetic: 0.96 us -> none  [per_device(): turn = jnp.concatenate([jnp.cos(spin), jnp.sin(spin)], 0)]
where the time goes in v2:
time: 60.9 us; the launch traced here: 60.5 us
  Pallas kernels  54.7 us (90%)
  local copies, waits for them, and re-layouts  5.15 us (8%)
  between operations  0.64 us (1%)
    pallas_call x1, Pallas kernels, run_fused(): pl.pallas_call(functools.partial(fused_kernel, (devices, count, cycles, a...  54.7 us
    unnamed x4, local copies, waits for them, and re-layouts  5.15 us

profile of v2, /device:TPU:0, one launch (start us, length us, event | category | flops | bytes accessed | tf_op | source)
XLA Modules:
  0.0 60.5 jit_solution(12505089216199534714)
XLA Ops:
  0.6 54.7 %shard_map.156 = (f32[16,128]{1,0:T(8,128)}, f32[1,128]{1,0:T(1,128)}, f32[1,32,256]{2,1,0:T(8,128)}, f32[1,32,256]{2,1,0:T(8,128)}) custom-call(s32[1,128]{1,0:T(1,128)} %bitcast.10, s32[1,128]{1,0:T(1,128)} %bitcast.11, s32[2,128]{1,0:T(2,128)} %bitcast.9, bf16[128,32,256]{2,1,0:T(8,128)(2,1)} %images_ref.1, bf16[192,128]{1,0:T(8,128)(2,1)} %bitcast.7, ...), custom_call_target="tpu_custom_call" | custom-call | tf_op jit(solution)/shard_map/pallas_call | solution.py:793
  55.4 1.3 %copy.21 = f32[128,16]{0,1:T(8,128)} copy(f32[128,16]{0,1:T(8,128)} %bitcast.8) | data formatting | bytes 16384
  56.7 1.1 %copy.22 = f32[128]{0:T(128)} copy(f32[128]{0:T(128)} %bitcast.13) | data formatting | bytes 1024
  57.8 1.4 %copy.23 = f32[1,32,256]{2,1,0:T(8,128)} copy(f32[1,32,256]{2,1,0:T(8,128)} %get-tuple-element.18) | data formatting | bytes 65536
  59.2 1.4 %copy.24 = f32[1,32,256]{2,1,0:T(8,128)} copy(f32[1,32,256]{2,1,0:T(8,128)} %get-tuple-element.19) | data formatting | bytes 65536

commit v3 on v2

--- a/solution.py
+++ b/solution.py
@@ -389,10 +389,10 @@
             gather_up(group * 8 + u)
 
 
-def fused_kernel(sizes, owner_ref, mic_ref, shift_ref, images_ref, ctf_ref, own_values_ref,
+def fused_kernel(sizes, owner_ref, mic_ref, shift_ref, particles_ref, ctf_ref, own_values_ref,
                  prior_ref, moves_ref, turns_ref, forward_ref, power_ref,
-                 rotate_ref, spread_ref, post_ref, evid_ref, numer_ref, denom_ref,
-                 all_ctf, all_refs, own_refs, work, table, phase, spec, refs, mixed, parts,
+                 rotate_ref, spread_ref, post_ref, evid_ref, total_ref,
+                 images_ref, images_sem, all_ctf, all_refs, own_refs, work, table, phase, spec, refs, mixed, parts,
                  near, side_out, side_in, layer_out, layer_in,
                  ctf_send, ctf_recv, refs_send, refs_recv, near_sems, side_sems, layer_sems):
     devices, count, cycles, angles = sizes
@@ -403,6 +403,8 @@
     chunk = angles // CHUNKS
     wide = chunk + PAD
 
+    fetch = pltpu.make_async_copy(particles_ref, images_ref, images_sem)
+    fetch.start()
     me, core, side, layer, layers = neighbours(devices)
     column = side * 2 + core
     sibling = me + 1 - 2 * core
@@ -490,6 +492,9 @@
     own_refs[...] = own_block
     all_refs[me] = own_block
     refs_begin()
+    table[...] = jnp.zeros_like(table)
+    parts[...] = jnp.zeros_like(parts)
+    fetch.wait()
 
     def spread_image(i):
         image = images_ref[i].astype(F32)
@@ -512,6 +517,10 @@
     held_rows = table.shape[0] // (cycles + PAD)
     picked = picks(held_rows, owner_ref[...] * mics + mic_ref[...]).T.astype(BF16)
 
+    chosen = picks(16, prior_ref[...])
+    chosen = jnp.concatenate([chosen, chosen, chosen, jnp.zeros_like(chosen)], 0).astype(BF16)
+    turn = dot(turns_ref[...], chosen)
+    turn_re, turn_im = turn[:angles], turn[angles:]
     steps = max(layers, 1)
     span = count // steps
 
@@ -526,16 +535,7 @@
             ctf_along(hop + 1)
     for hop in range(layers):
         ctf_over(hop)
-    for hop in range(1, layers):
-        refs_along(hop)
-
-    chosen = picks(16, prior_ref[...])
-    chosen = jnp.concatenate([chosen, chosen, chosen, jnp.zeros_like(chosen)], 0).astype(BF16)
-    turn = dot(turns_ref[...], chosen)
-    turn_re, turn_im = turn[:angles], turn[angles:]
     ctf_finish()
-
-    table[...] = jnp.zeros_like(table)
 
     @pl.loop(0, devices)
     def _(block):
@@ -583,7 +583,14 @@
         def _(group):
             transform(hop * part + group * 2)
 
-        refs_over(hop)
+        if hop == 0:
+            for other in range(1, layers):
+                refs_along(other)
+        if hop == max(steps - 2, 0):
+            for other in range(layers // 2):
+                refs_over(other)
+    for other in range(layers // 2, layers):
+        refs_over(other)
     refs_finish()
 
     def position(k):
@@ -720,7 +727,6 @@
             total = total + layer_in[number, hop]
         return total
 
-    parts[...] = jnp.zeros_like(parts)
     for number in range(CHUNKS):
 
         @pl.loop(0, chunk // 8)
@@ -737,13 +743,21 @@
     if CHUNKS >= 2:
         stage_layer(CHUNKS - 2)
     stage_layer(CHUNKS - 1)
-    turned = jnp.concatenate([stage_total(number) for number in range(CHUNKS)], 0).T
+    for number in range(CHUNKS):
+        total_ref[number * chunk : (number + 1) * chunk] = stage_total(number)
+    for copy in waiting:
+        copy.wait_send()
+
+
+def finish_kernel(post_in, evid_in, total_ref, post_ref, evid_ref, numer_ref, denom_ref):
+    cycles, angles = numer_ref.shape[1], numer_ref.shape[2] // 2
+    post_ref[...] = post_in[...]
+    evid_ref[...] = evid_in[...]
+    turned = total_ref[...].T
     numer_ref[0, :, :angles] = turned[:cycles]
     denom_ref[0, :, :angles] = turned[cycles : 2 * cycles]
     numer_ref[0, :, angles:] = turned[2 * cycles : 3 * cycles]
     denom_ref[0, :, angles:] = turned[3 * cycles :]
-    for copy in waiting:
-        copy.wait_send()
 
 
 def three(values):
@@ -790,17 +804,18 @@
     )
     sums = jax.ShapeDtypeStruct((1, cycles, 2 * angles), F32)
     dma = pltpu.SemaphoreType.DMA
-    post, evidence, numer, denom = pl.pallas_call(
+    scored = pl.pallas_call(
         functools.partial(fused_kernel, (devices, count, cycles, angles)),
         out_shape=(
             jax.ShapeDtypeStruct((classes, count), F32),
             jax.ShapeDtypeStruct((1, count), F32),
-            sums,
-            sums,
+            jax.ShapeDtypeStruct((angles, depth), F32),
         ),
-        in_specs=[VMEM] * 13,
-        out_specs=(VMEM,) * 4,
+        in_specs=[VMEM] * 3 + [pl.BlockSpec(memory_space=pl.ANY)] + [VMEM] * 9,
+        out_specs=(VMEM,) * 3,
         scratch_shapes=[
+            pltpu.VMEM(particles.shape, BF16),
+            dma,
             pltpu.VMEM((devices, mics * cycles, angles), BF16),
             pltpu.VMEM((devices, angles, depth), BF16),
             pltpu.VMEM((angles, depth), BF16),
@@ -829,6 +844,18 @@
         ),
     )(owner.reshape(1, count), mic_local.reshape(1, count), shifts.T, particles, ctf.reshape(mics * cycles, angles), refs,
       prior.reshape(1, count), *[jnp.asarray(constant) for constant in constants])
+    post, evidence, numer, denom = pl.pallas_call(
+        finish_kernel,
+        out_shape=(
+            jax.ShapeDtypeStruct((classes, count), F32),
+            jax.ShapeDtypeStruct((1, count), F32),
+            sums,
+            sums,
+        ),
+        in_specs=[VMEM] * 3,
+        out_specs=(VMEM,) * 4,
+        compiler_params=pltpu.CompilerParams(vmem_limit_bytes=60 * MIB),
+    )(*scored)
     return post.T, evidence[0], numer, denom
 
 

time: 60.9 us -> 56 us (0.920)
  local copies, waits for them, and re-layouts: 5.15 us -> 0 us
    unnamed x4 -> x0, local copies, waits for them, and re-layouts: 5.15 us -> none
    pallas_call x0 -> x1, Pallas kernels: none -> 1.58 us  [run_fused(): pl.pallas_call(finish_kernel, out_shape=(jax.ShapeDtypeStruct((classes, c...]
    pallas_call x1, Pallas kernels: 54.7 us -> 53.6 us  [run_fused(): pl.pallas_call(functools.partial(fused_kernel, (devices, count, cycles, a...]
where the time goes in v3:
time: 56 us; the launch traced here: 55.8 us
  Pallas kernels  55.1 us (98%)
  between operations  0.64 us (1%)
    pallas_call x1, Pallas kernels, run_fused(): pl.pallas_call(functools.partial(fused_kernel, (devices, count, cycles, a...  53.6 us
    pallas_call x1, Pallas kernels, run_fused(): pl.pallas_call(finish_kernel, out_shape=(jax.ShapeDtypeStruct((classes, c...  1.58 us

profile of v3, /device:TPU:0, one launch (start us, length us, event | category | flops | bytes accessed | tf_op | source)
XLA Modules:
  0.0 55.8 jit_solution(4792124473743635295)
XLA Ops:
  0.6 53.6 %shard_map.156 = (f32[16,128]{1,0:T(8,128)}, f32[1,128]{1,0:T(1,128)}, f32[128,128]{1,0:T(8,128)}) custom-call(s32[1,128]{1,0:T(1,128)} %bitcast.9, s32[1,128]{1,0:T(1,128)} %bitcast.10, s32[2,128]{1,0:T(2,128)} %bitcast.8, bf16[128,32,256]{2,1,0:T(8,128)(2,1)} %particles_ref.1, bf16[192,128]{1,0:T(8,128)(2,1)} %bitcast.7, ...), custom_call_target="tpu_custom_call" | custom-call | tf_op jit(solution)/shard_map/pallas_call | solution.py:807
  54.2 1.6 %shard_map.157 = (f32[16,128]{1,0:T(8,128)}, f32[1,128]{1,0:T(1,128)}, f32[1,32,256]{2,1,0:T(8,128)}, f32[1,32,256]{2,1,0:T(8,128)}) custom-call(f32[16,128]{1,0:T(8,128)} %get-tuple-element.11.post_in, f32[1,128]{1,0:T(1,128)} %get-tuple-element.12.evid_in, f32[128,128]{1,0:T(8,128)} %get-tuple-element.13.total_ref), custom_call_target="tpu_custom_call" | custom-call | tf_op jit(solution)/shard_map/pallas_call | solution.py:847

commit v4 on v3

--- a/solution.py
+++ b/solution.py
@@ -20,7 +20,7 @@
 SMEM = pl.BlockSpec(memory_space=pltpu.SMEM)
 MIB = 1 << 20
 PAD = 8
-CHUNKS = 4
+CHUNKS = 2
 
 
 def split_table(table):

time: 56 us -> 55 us (0.982)
  Pallas kernels: 55.1 us -> 54.1 us
    pallas_call x1, Pallas kernels: 53.6 us -> 52.5 us  [run_fused(): pl.pallas_call(functools.partial(fused_kernel, (devices, count, cycles, a...]
where the time goes in v4:
time: 55 us; the launch traced here: 54.8 us
  Pallas kernels  54.1 us (98%)
  between operations  0.64 us (1%)
    pallas_call x1, Pallas kernels, run_fused(): pl.pallas_call(functools.partial(fused_kernel, (devices, count, cycles, a...  52.5 us
    pallas_call x1, Pallas kernels, run_fused(): pl.pallas_call(finish_kernel, out_shape=(jax.ShapeDtypeStruct((classes, c...  1.58 us

profile of v4, /device:TPU:0, one launch (start us, length us, event | category | flops | bytes accessed | tf_op | source)
XLA Modules:
  0.0 54.8 jit_solution(11548238686662301145)
XLA Ops:
  0.6 52.5 %shard_map.156 = (f32[16,128]{1,0:T(8,128)}, f32[1,128]{1,0:T(1,128)}, f32[128,128]{1,0:T(8,128)}) custom-call(s32[1,128]{1,0:T(1,128)} %bitcast.9, s32[1,128]{1,0:T(1,128)} %bitcast.10, s32[2,128]{1,0:T(2,128)} %bitcast.8, bf16[128,32,256]{2,1,0:T(8,128)(2,1)} %particles_ref.1, bf16[192,128]{1,0:T(8,128)(2,1)} %bitcast.7, ...), custom_call_target="tpu_custom_call" | custom-call | tf_op jit(solution)/shard_map/pallas_call | solution.py:807
  53.2 1.6 %shard_map.157 = (f32[16,128]{1,0:T(8,128)}, f32[1,128]{1,0:T(1,128)}, f32[1,32,256]{2,1,0:T(8,128)}, f32[1,32,256]{2,1,0:T(8,128)}) custom-call(f32[16,128]{1,0:T(8,128)} %get-tuple-element.11.post_in, f32[1,128]{1,0:T(1,128)} %get-tuple-element.12.evid_in, f32[128,128]{1,0:T(8,128)} %get-tuple-element.13.total_ref), custom_call_target="tpu_custom_call" | custom-call | tf_op jit(solution)/shard_map/pallas_call | solution.py:847
